TPU v7x, 32 devices: a whole 2x2x4 slice. The times are simulated.
32 devices in a mesh: front: 4 (over y, x), blk: 8 (over z, core).
Axes of the slice: x: 2, y: 2, z: 4, core: 2. Of those that a mesh axis runs over, the one named last changes fastest.
Arguments:
- front_matrix: float32 [4, 13312, 13312], P('front', 'blk')
- random_probe: float32 [4, 13312, 256], P('front', 'blk'), may hold values from -6 to 6
- child_samples: float32 [4, 3072, 256], P('front', 'blk'), may hold values from -6 to 6
- child_dest: int32 [4, 3072], P('front', 'blk'), may hold values from 0 to 13311, as said below
- skeleton: int32 [4, 8, 128], P('front', 'blk'), may hold values from 0 to 1663, as said below
- leaf_ranks: int32 [4, 8], P('front', 'blk'), may hold values from 64 to 128, as said below
- pair_skeleton: int32 [4, 4, 128], P('front'), may hold values from 0 to 255, as said below
Outputs:
- interp_leaf: float32 [4, 13312, 128], P('front', 'blk')
- interp_pair: float32 [4, 1024, 128], P('front', 'blk')
Inputs may be any that keep to these rules, and one draw needn't show every extreme that they name: `child_dest`: among the rows of one device, at most 96 name rows of one leaf node; in every group one leaf node of the next group receives exactly 96 rows from every device of the group. `skeleton`: the 128 entries of one leaf are distinct. `leaf_ranks`: 128 is reached in every front. `pair_skeleton`: the 128 entries of one node are distinct and name live slots only: k of leaf 2q with k below its rank, or 128 + k of leaf 2q+1 with k below its rank.
All inputs are finite; a program needn't handle non-finite values.
Results may differ from a plain program's by a relative error of at most 0.0003.
Values sent between devices are 32-bit elements; how exact they have to be, the bound alone decides.
A program may use at most 192 MiB of HBM per device.

v0:
```python
import jax
import jax.numpy as jnp
from jax import lax
from jax.sharding import PartitionSpec as P

HIGHEST = lax.Precision.HIGHEST
ridge_share = 0.1


def from_behind(value, axis, steps):
    count = lax.axis_size(axis)
    pairs = [(source, (source + steps) % count) for source in range(count)]
    return lax.ppermute(value, axis, pairs)


def from_partner(value, axis, stride):
    mask = 2**stride
    pairs = [(source, source ^ mask) for source in range(lax.axis_size(axis))]
    return lax.ppermute(value, axis, pairs)


def exact_dot(left, right):
    return jnp.dot(left, right, precision=HIGHEST, preferred_element_type=jnp.float32)


def interpolate(targets, leaf_basis, live_mask, live_count):
    gram_matrix = exact_dot(leaf_basis, leaf_basis.T)
    ridge_size = ridge_share * jnp.sum(jnp.diagonal(gram_matrix)) / live_count
    gram_matrix = gram_matrix + jnp.diag(jnp.where(live_mask, ridge_size, 1.0))
    factor = jnp.linalg.cholesky(gram_matrix)
    cross_terms = exact_dot(targets, leaf_basis.T)
    return jax.scipy.linalg.cho_solve((factor, True), cross_terms.T).T


def body(
    front_matrix, random_probe, child_samples, child_dest, skeleton, leaf_ranks, pair_skeleton
):
    matrix = front_matrix[0]
    own_probe = random_probe[0]
    height = matrix.shape[0]
    samples = own_probe.shape[1]
    leaf_index = lax.axis_index("blk")
    pair_index = leaf_index // 2
    lower_half = leaf_index % 2 == 0
    pair_start = pair_index * (2 * height)
    piece_rows = lax.all_gather(own_probe, "blk", axis=0, tiled=True)
    pair_probe = jnp.zeros((2 * height, samples), jnp.float32)
    piece_count = piece_rows.shape[0]
    product = exact_dot(matrix, piece_rows)
    offsets = jnp.arange(piece_count, dtype=jnp.int32) - pair_start
    inside = (offsets >= 0) & (offsets < 2 * height)
    pair_probe = pair_probe.at[jnp.where(inside, offsets, 2 * height)].set(piece_rows, mode="drop")
    product, pair_probe = (product, pair_probe)
    blocks = lax.axis_size("blk")
    incoming = child_samples[0]
    destinations = child_dest[0]
    count_rows = incoming.shape[0]
    capacity = max(2, (2 * count_rows + blocks - 1) // blocks)
    owner_block = destinations // height
    within = (destinations % height).astype(jnp.float32)
    onehot = (owner_block[:, None] == jnp.arange(blocks, dtype=jnp.int32)[None, :]).astype(
        jnp.int32
    )
    ranking = jnp.sum(jnp.cumsum(onehot, axis=0) * onehot, axis=1) - 1
    places = owner_block * capacity + ranking
    slots_total = blocks * capacity
    sending = jnp.zeros((slots_total, samples), jnp.float32).at[places].set(incoming)
    labels = jnp.full((slots_total,), float(height), jnp.float32).at[places].set(within)
    spread_rows, spread_labels = (
        lax.all_to_all(sending, "blk", split_axis=0, concat_axis=0, tiled=True),
        lax.all_to_all(labels, "blk", split_axis=0, concat_axis=0, tiled=True),
    )
    arrived, arrived_labels = from_behind((spread_rows, spread_labels), "front", 1)
    child_part = jax.ops.segment_sum(
        arrived, arrived_labels.astype(jnp.int32), num_segments=height + 1
    )[:height]
    sample = product + child_part
    diagonal_block = lax.dynamic_slice_in_dim(matrix, leaf_index * height, height, 1)
    off_sample = sample - exact_dot(diagonal_block, own_probe)
    chosen = skeleton[0, 0]
    leaf_rank = leaf_ranks[0, 0]
    live_mask = jnp.arange(chosen.shape[0]) < leaf_rank
    leaf_basis = off_sample[chosen] * live_mask[:, None]
    leaf_interp = interpolate(off_sample, leaf_basis, live_mask, leaf_rank.astype(jnp.float32))
    pair_columns = lax.dynamic_slice_in_dim(matrix, pair_start, 2 * height, 1)[chosen]
    upward = (sample[chosen] - exact_dot(pair_columns, pair_probe)) * live_mask[:, None]
    sibling = from_partner(upward, "blk", 0)
    stacked = jnp.where(
        lower_half, jnp.concatenate([upward, sibling]), jnp.concatenate([sibling, upward])
    )
    pick_rows = lax.dynamic_index_in_dim(pair_skeleton[0], pair_index, 0, keepdims=False)
    pair_basis = stacked[pick_rows]
    pair_width = pick_rows.shape[0]
    pair_interp = interpolate(
        upward, pair_basis, jnp.ones((pair_width,), jnp.bool_), float(pair_width)
    )
    return (leaf_interp[None], pair_interp[None])


def solution(mesh):
    placed = (
        P("front", "blk", None),
        P("front", "blk", None),
        P("front", "blk", None),
        P("front", "blk"),
        P("front", "blk", None),
        P("front", "blk"),
        P("front", None, None),
    )
    return jax.shard_map(
        body,
        mesh=mesh,
        in_specs=placed,
        out_specs=(P("front", "blk", None), P("front", "blk", None)),
        check_vma=False,
    )
```

profile of v0, /device:TPU:0, one launch (start us, length us, event | category | flops | bytes accessed | tf_op | source)
XLA Modules:
  0.0 379.3 jit_solution(6207482387478912908)
XLA Ops:
  11.3 2.7 scatter_custom_fusion.1
  14.0 6.3 %all-to-all-start.1 = ((f32[8,96,256]{2,1,0:T(8,128)}), f32[8,96,256]{2,1,0:T(8,128)S(1)}, u32[]{:S(2)}, u32[]{:S(2)}) async-start(f32[8,96,256]{2,1,0:T(8,128)} %bitcast.8), calls=%async_computation.1 | async-start | bytes 1572864 | tf_op jit(solution)/shard_map/all_to_all | solution.py:70
  20.4 2.9 scatter_custom_fusion
  24.0 16.3 %dynamic-slice_bitcast_fusion = f32[1664,3328]{1,0:T(8,128)} fusion(f32[1,1664,13312]{2,1,0:T(8,128)} %param.8, s32[]{:T(128)S(6)} %select_n.148), kind=kLoop, calls=%fused_computation.12 | loop fusion | bytes 44302340 | tf_op jit(solution)/shard_map/dynamic_slice | solution.py:85
  40.3 22.8 %all-to-all-done.1 = f32[8,96,256]{2,1,0:T(8,128)S(1)} async-done(((f32[8,96,256]{2,1,0:T(8,128)}), f32[8,96,256]{2,1,0:T(8,128)S(1)}, u32[]{:S(2)}, u32[]{:S(2)}) %all-to-all-start.1) | async-done | bytes 786464 | tf_op jit(solution)/shard_map/all_to_all | solution.py:70
  63.0 3.3 all-to-all-start
  66.4 1.5 collective-permute-start.1
  69.4 2.4 all-to-all-done
  73.1 1.5 collective-permute-start
  74.6 10.5 %gather_fusion.3 = f32[128,3328]{1,0:T(8,128)} fusion(f32[1664,3328]{1,0:T(8,128)} %dynamic-slice_bitcast_fusion, s32[1024]{0:T(1024)S(1)} %pad_clamp_fusion.1), kind=kCustom, calls=%fused_computation.3 | custom fusion | bytes 3408384 | tf_op jit(solution)/shard_map/gather | solution.py:85
  85.1 2.1 collective-permute-done
  87.2 7.8 %scatter_custom_fusion.2 = f32[1665,256]{1,0:T(8,128)} fusion(s32[768]{0:T(1024)S(1)} %convert_element_type.25, f32[768,256]{1,0:T(8,128)S(1)} %collective-permute-done.1, f32[]{:T(128)} %constant.134.clone.1), kind=kCustom, calls=%fused_computation.25 | custom fusion | flops 196608 | bytes 1704964 | tf_op jit(solution)/shard_map/scatter-add | solution.py:74
  95.0 58.1 %all-gather.3.cloned.1.call-done = f32[1,13312,256]{2,1,0:T(8,128)} async-done(((f32[1,1664,256]{2,1,0:T(8,128)}), f32[1,13312,256]{2,1,0:T(8,128)}) %all-gather.3.cloned.1.call-update) | async-done | bytes 13631504 | tf_op jit(solution)/shard_map/all_gather | solution.py:46
  153.1 80.6 %slice_add_fusion = f32[1664,256]{1,0:T(8,128)S(1)} fusion(f32[1665,256]{1,0:T(8,128)} %scatter_custom_fusion.2, f32[1,13312,256]{2,1,0:T(8,128)} %all-gather.3.cloned.1.call-done, f32[1,1664,13312]{2,1,0:T(8,128)} %param.8), kind=kOutput, calls=%fused_computation.21 | convolution fusion | flops 68048814080 | bytes 105644032 | tf_op jit(solution)/shard_map/dot_general | solution.py:23
  235.6 13.5 %fusion.8 = f32[1664,256]{1,0:T(8,128)S(1)} fusion(f32[1664,256]{1,0:T(8,128)} %copy-done.1, f32[1,1664,13312]{2,1,0:T(8,128)} %param.8, s32[]{:T(128)S(6)} %select_n.141, f32[1,1664,256]{2,1,0:T(8,128)} %param.9), kind=kOutput, calls=%fused_computation.19 | convolution fusion | flops 8506474496 | bytes 16187396 | tf_op jit(solution)/shard_map/dot_general | solution.py:23
  250.2 1.7 fusion.18
  252.0 58.4 %scatter_custom_fusion.3 = f32[3328,256]{1,0:T(8,128)} fusion(s32[13312]{0:T(1024)S(1)} %bitcast.109, f32[1,13312,256]{2,1,0:T(8,128)} %all-gather.3.cloned.1.call-done, f32[]{:T(128)} %constant.134.clone.1), kind=kCustom, calls=%fused_computation.13 | custom fusion | bytes 17039364 | tf_op jit(solution)/shard_map/scatter | solution.py:52
  310.4 3.7 fusion.52
  317.6 11.7 %cholesky.44 = f32[128,128]{1,0:T(8,128)S(1)} custom-call(f32[128,128]{1,0:T(8,128)S(1)} %copy.19), custom_call_target="Cholesky" | custom-call | tf_op jit(solution)/shard_map/jit(cholesky)/cholesky | solution.py:30
  330.7 9.8 %custom-call.16 = f32[1,128,128]{1,2,0:T(8,128)S(1)} custom-call(f32[1,128,128]{2,1,0:T(8,128)S(1)} %fusion.22), custom_call_target="InvertDiagBlocksLowerTriangular" | custom-call | tf_op jit(solution)/shard_map/jit(_cho_solve)/triangular_solve | solution.py:32
  341.4 2.4 convolution_bitcast_fusion
  345.2 1.5 gather_fusion.5
  348.1 11.7 %cholesky.55 = f32[128,128]{1,0:T(8,128)S(1)} custom-call(f32[128,128]{1,0:T(8,128)S(1)} %copy.21), custom_call_target="Cholesky" | custom-call | tf_op jit(solution)/shard_map/jit(cholesky)/cholesky | solution.py:30
  361.2 9.8 %custom-call.17 = f32[1,128,128]{1,2,0:T(8,128)S(1)} custom-call(f32[1,128,128]{2,1,0:T(8,128)S(1)} %fusion.23), custom_call_target="InvertDiagBlocksLowerTriangular" | custom-call | tf_op jit(solution)/shard_map/jit(_cho_solve)/triangular_solve | solution.py:32
  (65 shorter events, 19.6 us)
Async XLA Ops:
  7.2 4.1 %copy-start = (f32[1,384,256]{2,1,0:T(8,128)S(1)}, f32[1,384,256]{2,1,0:T(8,128)}, u32[]{:S(2)}) copy-start(f32[1,384,256]{2,1,0:T(8,128)} %param.10) | copy-start | bytes 1179652
  7.2 145.9 %all-gather.3.cloned.1.call-start = ((), (), s32[]{:S(2)}) async-start(), calls=%async_computation.2 | async-start | bytes 15335424 | tf_op jit(solution)/shard_map/all_gather | solution.py:46
  14.0 49.0 %all-to-all-start.1 = ((f32[8,96,256]{2,1,0:T(8,128)}), f32[8,96,256]{2,1,0:T(8,128)S(1)}, u32[]{:S(2)}, u32[]{:S(2)}) async-start(f32[8,96,256]{2,1,0:T(8,128)} %bitcast.8), calls=%async_computation.1 | async-start | bytes 1572864 | tf_op jit(solution)/shard_map/all_to_all | solution.py:70
  24.0 44.8 %copy-start.3 = (s32[1,1,128]{2,1,0:T(1,128)S(1)}, s32[1,1,128]{2,1,0:T(1,128)}, u32[]{:S(2)}) copy-start(s32[1,1,128]{2,1,0:T(1,128)} %param.12) | copy-start | bytes 1540
  63.0 8.8 %all-to-all-start = ((f32[8,96,1]{1,2,0:T(1,128)}), f32[8,96,1]{1,2,0:T(1,128)S(1)}, u32[]{:S(2)}, u32[]{:S(2)}) async-start(f32[8,96,1]{1,2,0:T(1,128)} %bitcast.6), calls=%async_computation | async-start | bytes 8192 | tf_op jit(solution)/shard_map/all_to_all | solution.py:71
  66.4 20.8 %collective-permute-start.1 = (f32[768,256]{1,0:T(8,128)S(1)}, f32[768,256]{1,0:T(8,128)S(1)}, u32[]{:S(2)}, u32[]{:S(2)}) collective-permute-start(f32[768,256]{1,0:T(8,128)S(1)} %bitcast.108), channel_id=1, source_target_pairs={{0,8},{8,16},{16,24},{24,0},{1,9},{9,17},{17,25},{25,1},{2,10},{10... | collective-permute-start | bytes 2359304 | tf_op jit(solution)/shard_map/ppermute | solution.py:13
  73.1 14.1 %collective-permute-start = (f32[768]{0:T(1024)S(1)}, f32[768]{0:T(1024)S(1)}, u32[]{:S(2)}, u32[]{:S(2)}) collective-permute-start(f32[768]{0:T(1024)S(1)} %all_to_all.18), channel_id=1, source_target_pairs={{0,8},{8,16},{16,24},{24,0},{1,9},{9,17},{17,25},{25,1},{2,10},{10... | collective-permute-start | bytes 9224 | tf_op jit(solution)/shard_map/ppermute | solution.py:13
  233.7 1.2 copy-start.1
  252.0 58.4 %copy-start.2 = (f32[128,3328]{1,0:T(8,128)S(1)}, f32[128,3328]{1,0:T(8,128)}, u32[]{:S(2)}) copy-start(f32[128,3328]{1,0:T(8,128)} %gather_fusion.3) | copy-start | bytes 5111812
  314.2 29.6 %collective-permute-start.2 = (f32[128,256]{1,0:T(8,128)S(1)}, f32[128,256]{1,0:T(8,128)S(1)}, u32[]{:S(2)}, u32[]{:S(2)}) collective-permute-start(f32[128,256]{1,0:T(8,128)S(1)} %subtract_multiply_fusion), channel_id=1, source_target_pairs={{0,1},{1,0},{2,3},{3,2},{4,5},{5,4},{6,7},{7,6},{8,9},{9,8},{10,11... | collective-permute-start | bytes 393224 | tf_op jit(solution)/shard_map/ppermute | solution.py:19
Sparse Core Ops, SparseCore 0:
  9.7 143.3 all-gather.2
where the time goes:
time: 386 us; the launch traced here: 379 us
  matrix products  105 us (27%)
  local copies, waits for them, and re-layouts  99 us (26%)
  waiting for transfers between devices  86.1 us (22%)
  other arithmetic  59.7 us (15%)
  between operations  16.6 us (4%)
  starting transfers between devices  13 us (3%)
    dot_general x7, matrix products, exact_dot(): jnp.dot(left, right, precision=HIGHEST, preferred_element_type=jnp.float32)  100 us
    scatter x1, local copies, waits for them, and re-layouts, body(): pair_probe.at[jnp.where(inside, offsets, 2 * height)]  58.4 us
    all_gather x1, waiting for transfers between devices, body(): piece_rows = lax.all_gather(own_probe, 'blk', axis=0, tiled=True)  58.1 us
    another operation x6, other arithmetic, interpolate(): factor = jnp.linalg.cholesky(gram_matrix)  24.8 us
    all_to_all x1, waiting for transfers between devices, body(): lax.all_to_all(sending, 'blk', split_axis=0, concat_axis=0, tiled=True)  22.8 us
    another operation x4, other arithmetic, interpolate(): return jax.scipy.linalg.cho_solve((factor, True), cross_terms.T).T  20.9 us
    dynamic_slice x1, local copies, waits for them, and re-layouts, body(): lax.dynamic_slice_in_dim(matrix, pair_start, 2 * height, 1)[chosen]  16.3 us
    gather x1, local copies, waits for them, and re-layouts, body(): lax.dynamic_slice_in_dim(matrix, pair_start, 2 * height, 1)[chosen]  10.5 us
  transfers between devices with their start and end apart: 6, of which 4 were waited for; matrix products, arithmetic and copies ran while one was open for 20% of the time, Pallas kernels for 0%

commit v1 on v0

v1 whole, which is shorter than its diff:
```python
import functools

import jax
import jax.numpy as jnp
from jax import lax
from jax.experimental import pallas as pl
from jax.experimental.pallas import tpu as pltpu
from jax.sharding import PartitionSpec as P

HIGHEST = lax.Precision.HIGHEST
ridge_share = 0.1


def from_behind(value, axis, steps):
    count = lax.axis_size(axis)
    pairs = [(source, (source + steps) % count) for source in range(count)]
    return lax.ppermute(value, axis, pairs)


def from_partner(value, axis, stride):
    mask = 2**stride
    pairs = [(source, source ^ mask) for source in range(lax.axis_size(axis))]
    return lax.ppermute(value, axis, pairs)


def exact_dot(left, right):
    return jnp.dot(left, right, precision=HIGHEST, preferred_element_type=jnp.float32)


def divisor(total, unit, most):
    return max(d for d in range(unit, most + 1, unit) if total % d == 0)


def halves(value):
    high = value.astype(jnp.bfloat16)
    return high, (value - high.astype(jnp.float32)).astype(jnp.bfloat16)


def transposed_kernel(height, sub, me_ref, probe_ref, matrix_ref, out_ref, cat_ref):
    step = pl.program_id(0)
    half = probe_ref.shape[0]
    tile = matrix_ref.shape[1]

    @pl.when(step == 0)
    def _():
        high, low = halves(probe_ref[...])
        cat_ref[pl.ds(0, half), :] = high
        cat_ref[pl.ds(half, half), :] = low

    first = me_ref[0] * height

    def column(index, carry):
        start = pl.multiple_of(index * sub, sub)
        high, low = halves(matrix_ref[:, pl.ds(start, sub)])
        cat = cat_ref[...]
        part = jnp.dot(cat, high, preferred_element_type=jnp.float32)
        part = part + jnp.dot(cat, low, preferred_element_type=jnp.float32)
        rows = (part[:half] + part[half:]).T
        place = step * tile + start + lax.broadcasted_iota(jnp.int32, rows.shape, 0)
        own = (place >= first) & (place < first + height)
        out_ref[pl.ds(start, sub), :] = jnp.where(own, 0.0, rows)
        return carry

    lax.fori_loop(0, tile // sub, column, 0)


def transposed_product(matrix, probe_t, me):
    height, width = matrix.shape
    half = probe_t.shape[0]
    tile = divisor(width, 256, 1024)
    sub = 256
    return pl.pallas_call(
        functools.partial(transposed_kernel, height, sub),
        grid=(width // tile,),
        in_specs=[
            pl.BlockSpec(memory_space=pltpu.SMEM),
            pl.BlockSpec((half, height), lambda i: (0, 0)),
            pl.BlockSpec((height, tile), lambda i: (0, i)),
        ],
        out_specs=pl.BlockSpec((tile, half), lambda i: (i, 0)),
        out_shape=jax.ShapeDtypeStruct((width, half), jnp.float32),
        scratch_shapes=[pltpu.VMEM((2 * half, height), jnp.bfloat16)],
        compiler_params=pltpu.CompilerParams(vmem_limit_bytes=48 * 2**20),
        cost_estimate=pl.CostEstimate(
            flops=8 * height * width * half,
            bytes_accessed=4 * height * width,
            transcendentals=0,
        ),
        name="transposed_product",
    )(me, probe_t, matrix)


def forward_kernel(height, chunk, me_ref, probe_ref, matrix_ref, out_ref, total_ref, cat_ref):
    step = pl.program_id(0)
    tile, half = probe_ref.shape
    first = me_ref[0] * height
    place = step * tile + lax.broadcasted_iota(jnp.int32, (tile, half), 0)
    own = (place >= first) & (place < first + height)
    probe_high, probe_low = halves(jnp.where(own, 0.0, probe_ref[...]))
    cat_ref[:, pl.ds(0, half)] = probe_high
    cat_ref[:, pl.ds(half, half)] = probe_low

    @pl.when(step == 0)
    def _():
        total_ref[...] = jnp.zeros_like(total_ref)

    def rows(index, carry):
        span = pl.ds(pl.multiple_of(index * chunk, chunk), chunk)
        high, low = halves(matrix_ref[span, :])
        cat = cat_ref[...]
        part = jnp.dot(high, cat, preferred_element_type=jnp.float32)
        part = part + jnp.dot(low, cat, preferred_element_type=jnp.float32)
        total_ref[span, :] += part
        return carry

    lax.fori_loop(0, height // chunk, rows, 0)

    @pl.when(step == pl.num_programs(0) - 1)
    def _():
        out_ref[...] = total_ref[:, pl.ds(0, half)] + total_ref[:, pl.ds(half, half)]


def forward_product(matrix, probe, me):
    height, width = matrix.shape
    half = probe.shape[1]
    tile = divisor(width, 256, 1024)
    chunk = divisor(height, 16, 512)
    return pl.pallas_call(
        functools.partial(forward_kernel, height, chunk),
        grid=(width // tile,),
        in_specs=[
            pl.BlockSpec(memory_space=pltpu.SMEM),
            pl.BlockSpec((tile, half), lambda i: (i, 0)),
            pl.BlockSpec((height, tile), lambda i: (0, i)),
        ],
        out_specs=pl.BlockSpec((height, half), lambda i: (0, 0)),
        out_shape=jax.ShapeDtypeStruct((height, half), jnp.float32),
        scratch_shapes=[
            pltpu.VMEM((height, 2 * half), jnp.float32),
            pltpu.VMEM((tile, 2 * half), jnp.bfloat16),
        ],
        compiler_params=pltpu.CompilerParams(vmem_limit_bytes=48 * 2**20),
        cost_estimate=pl.CostEstimate(
            flops=8 * height * width * half,
            bytes_accessed=4 * height * width,
            transcendentals=0,
        ),
        name="forward_product",
    )(me, probe, matrix)


def last_dims(left, right):
    return lax.dot_general(
        left,
        right,
        (((1,), (1,)), ((), ())),
        precision=HIGHEST,
        preferred_element_type=jnp.float32,
    )


def ridged(basis, live, count, row_ids, lane_ids):
    gram = last_dims(basis, basis)
    diagonal = row_ids == lane_ids
    trace = jnp.sum(jnp.where(diagonal, gram, 0.0))
    ridge = ridge_share * trace / count
    return gram + jnp.where(diagonal, jnp.where(row_ids < live, ridge, 1.0), 0.0)


def eliminate(state, k, row_ids, lane_ids):
    at_row = row_ids == k
    at_lane = lane_ids == k
    row = jnp.sum(jnp.where(at_row, state, 0.0), axis=0, keepdims=True)
    column = jnp.sum(jnp.where(at_lane, state, 0.0), axis=1, keepdims=True)
    pivot = jnp.sum(jnp.where(at_lane[:1], row, 0.0), axis=1, keepdims=True)
    inverse = 1.0 / pivot
    row = jnp.where(at_lane[:1], inverse, row * inverse)
    rest = jnp.where(at_lane, 0.0, state) - column * row
    return jnp.where(at_row, row, rest)


def interpolate_kernel(
    rank_ref, off_ref, basis_ref, upward_ref, pair_ref, leaf_out_ref, pair_out_ref
):
    slots = basis_ref.shape[0]
    width = pair_ref.shape[0]
    rank = rank_ref[0]
    row_ids = lax.broadcasted_iota(jnp.int32, (slots, slots), 0)
    lane_ids = lax.broadcasted_iota(jnp.int32, (slots, slots), 1)
    basis = basis_ref[...]
    pair = pair_ref[...]
    leaf_state = ridged(basis, rank, rank.astype(jnp.float32), row_ids, lane_ids)
    pair_state = ridged(pair, width, float(width), row_ids, lane_ids)

    def step(k, states):
        return tuple(eliminate(state, k, row_ids, lane_ids) for state in states)

    leaf_state, pair_state = lax.fori_loop(0, slots, step, (leaf_state, pair_state))
    leaf_weights = jnp.dot(
        leaf_state, basis, precision=HIGHEST, preferred_element_type=jnp.float32
    )
    pair_weights = jnp.dot(pair_state, pair, precision=HIGHEST, preferred_element_type=jnp.float32)
    pair_out_ref[...] = last_dims(upward_ref[...], pair_weights)
    leaf_out_ref[...] = last_dims(off_ref[...], leaf_weights)


def interpolate_both(rank, off, basis, upward, pair):
    vmem = pl.BlockSpec(memory_space=pltpu.VMEM)
    return pl.pallas_call(
        interpolate_kernel,
        in_specs=[pl.BlockSpec(memory_space=pltpu.SMEM)] + [vmem] * 4,
        out_specs=[vmem] * 2,
        out_shape=[
            jax.ShapeDtypeStruct((off.shape[0], basis.shape[0]), jnp.float32),
            jax.ShapeDtypeStruct((upward.shape[0], pair.shape[0]), jnp.float32),
        ],
        compiler_params=pltpu.CompilerParams(vmem_limit_bytes=32 * 2**20),
        name="interpolate_both",
    )(rank, off, basis, upward, pair)


def body(
    front_matrix, random_probe, child_samples, child_dest, skeleton, leaf_ranks, pair_skeleton
):
    matrix = front_matrix[0]
    own_probe = random_probe[0]
    height = matrix.shape[0]
    samples = own_probe.shape[1]
    half = samples // 2
    leaf_index = lax.axis_index("blk")
    me = leaf_index.astype(jnp.int32)[None]
    pair_index = leaf_index // 2
    lower_half = leaf_index % 2 == 0

    gathered = lax.all_gather(own_probe[:, :half], "blk", axis=0, tiled=True)
    partial = transposed_product(matrix, own_probe[:, half:].T, me)
    upper_columns = lax.psum_scatter(partial, "blk", scatter_dimension=0, tiled=True)
    sibling_probe = from_partner(own_probe, "blk", 0)

    blocks = lax.axis_size("blk")
    incoming = child_samples[0]
    destinations = child_dest[0]
    count_rows = incoming.shape[0]
    capacity = max(2, (2 * count_rows + blocks - 1) // blocks)
    owner_block = destinations // height
    within = (destinations % height).astype(jnp.float32)
    order = jnp.arange(count_rows, dtype=jnp.int32)
    earlier = (owner_block[:, None] == owner_block[None, :]) & (order[None, :] < order[:, None])
    ranking = jnp.sum(earlier.astype(jnp.int32), axis=1)
    places = owner_block * capacity + ranking
    slots_total = blocks * capacity
    sending = jnp.zeros((slots_total, samples), jnp.float32).at[places].set(incoming)
    labels = jnp.full((slots_total,), float(height), jnp.float32).at[places].set(within)
    spread_rows, spread_labels = (
        lax.all_to_all(sending, "blk", split_axis=0, concat_axis=0, tiled=True),
        lax.all_to_all(labels, "blk", split_axis=0, concat_axis=0, tiled=True),
    )
    arrived, arrived_labels = from_behind((spread_rows, spread_labels), "front", 1)
    child_part = jax.ops.segment_sum(
        arrived, arrived_labels.astype(jnp.int32), num_segments=height + 1
    )[:height]

    chosen = skeleton[0, 0]
    leaf_rank = leaf_ranks[0, 0]
    live_mask = (jnp.arange(chosen.shape[0]) < leaf_rank)[:, None]
    sibling_start = (leaf_index ^ 1) * height
    sibling_columns = lax.dynamic_slice_in_dim(matrix[chosen], sibling_start, height, 1)
    sibling_term = exact_dot(sibling_columns, sibling_probe)

    lower_columns = forward_product(matrix, gathered, me)
    off_sample = jnp.concatenate([lower_columns, upper_columns], axis=1) + child_part
    picked = off_sample[chosen]
    leaf_basis = jnp.where(live_mask, picked, 0.0)
    upward = jnp.where(live_mask, picked - sibling_term, 0.0)
    sibling = from_partner(upward, "blk", 0)
    stacked = jnp.where(
        lower_half, jnp.concatenate([upward, sibling]), jnp.concatenate([sibling, upward])
    )
    pick_rows = lax.dynamic_index_in_dim(pair_skeleton[0], pair_index, 0, keepdims=False)
    pair_basis = stacked[pick_rows]
    leaf_interp, pair_interp = interpolate_both(
        leaf_rank[None], off_sample, leaf_basis, upward, pair_basis
    )
    return (leaf_interp[None], pair_interp[None])


def solution(mesh):
    placed = (
        P("front", "blk", None),
        P("front", "blk", None),
        P("front", "blk", None),
        P("front", "blk"),
        P("front", "blk", None),
        P("front", "blk"),
        P("front", None, None),
    )
    return jax.shard_map(
        body,
        mesh=mesh,
        in_specs=placed,
        out_specs=(P("front", "blk", None), P("front", "blk", None)),
        check_vma=False,
    )
```

time: 386 us -> 221 us (0.57); the launches traced: 379 us -> 220 us
  Pallas kernels: 0 us -> 106 us
  matrix products: 105 us -> 3.4 us
  waiting for transfers between devices: 86.1 us -> 5.35 us
  local copies, waits for them, and re-layouts: 99 us -> 33 us
  other arithmetic: 59.7 us -> 11.2 us
  blocking collectives: 0 us -> 39.7 us
  starting transfers between devices: 13 us -> 6.62 us
    pallas_call x0 -> x3, Pallas kernels: none -> 106 us  [the longest x1 44.4 us: transposed_product(): pl.pallas_call(functools.partial(transposed_kernel, height, sub), grid=(w...]
    dot_general x7 -> x1, matrix products: 100 us -> 3.4 us  [exact_dot(): jnp.dot(left, right, precision=HIGHEST, preferred_element_type=jnp.float32)]
    scatter x1 -> x0, local copies, waits for them, and re-layouts: 58.4 us -> none  [body(): pair_probe.at[jnp.where(inside, offsets, 2 * height)]]
    all_gather x1, waiting for transfers between devices: 58.1 us -> 0.01 us  [body(): gathered = lax.all_gather(own_probe[:, :half], 'blk', axis=0, tiled=True)]
    another operation x12 -> x0, other arithmetic: 46.6 us -> none  [the longest x6 24.8 us: interpolate(): factor = jnp.linalg.cholesky(gram_matrix)]
    all_to_all x0 -> x1, blocking collectives: none -> 39.7 us  [body(): lax.all_to_all(sending, 'blk', split_axis=0, concat_axis=0, tiled=True)]
    all_to_all x1 -> x0, waiting for transfers between devices: 22.8 us -> none  [body(): lax.all_to_all(sending, 'blk', split_axis=0, concat_axis=0, tiled=True)]
    dynamic_slice x1 -> x0, local copies, waits for them, and re-layouts: 16.3 us -> none  [body(): lax.dynamic_slice_in_dim(matrix, pair_start, 2 * height, 1)[chosen]]
  transfers between devices with their start and end apart: 6 -> 7, of which waited for: 4 -> 2; matrix products, arithmetic and copies ran while one was open for 20% -> 17% of each run, Pallas kernels for 0% -> 39%
where the time goes in v1:
time: 221 us; the launch traced here: 220 us
  Pallas kernels  106 us (48%)
  blocking collectives  39.7 us (18%)
  local copies, waits for them, and re-layouts  33 us (15%)
  between operations  14.8 us (7%)
  other arithmetic  11.2 us (5%)
  starting transfers between devices  6.62 us (3%)
  waiting for transfers between devices  5.35 us (2%)
  matrix products  3.4 us (2%)
    pallas_call x1, Pallas kernels, transposed_product(): pl.pallas_call(functools.partial(transposed_kernel, height, sub), grid=(w...  44.4 us
    pallas_call x1, Pallas kernels, forward_product(): pl.pallas_call(functools.partial(forward_kernel, height, chunk), grid=(wi...  41.3 us
    all_to_all x1, blocking collectives, body(): lax.all_to_all(sending, 'blk', split_axis=0, concat_axis=0, tiled=True)  39.7 us
    pallas_call x1, Pallas kernels, interpolate_both(): pl.pallas_call(interpolate_kernel, in_specs=[pl.BlockSpec(memory_space=pl...  20 us
    gather x1, local copies, waits for them, and re-layouts, body(): matrix[chosen]  11.1 us
    all_gather x1, local copies, waits for them, and re-layouts, body(): gathered = lax.all_gather(own_probe[:, :half], 'blk', axis=0, tiled=True)  8.38 us
    scatter-add x1, other arithmetic, body(): jax.ops.segment_sum(arrived, arrived_labels.astype(jnp.int32), num_segmen...  7.57 us
  transfers between devices with their start and end apart: 7, of which 2 were waited for; matrix products, arithmetic and copies ran while one was open for 17% of the time, Pallas kernels for 39%

profile of v1, /device:TPU:0, one launch (start us, length us, event | category | flops | bytes accessed | tf_op | source)
XLA Modules:
  0.0 220.0 jit_solution(1778024569484541962)
XLA Ops:
  7.2 2.8 %copy.16 = f32[1,1664,256]{1,2,0:T(8,128)} copy(f32[1,1664,256]{2,1,0:T(8,128)} %param.8) | data formatting | bytes 3407872 | tf_op args[1]
  10.0 2.4 %fusion.18 = (f32[1664,128]{0,1:T(8,128)}, f32[128,1664]{1,0:T(8,128)S(1)}) fusion(f32[1664,256]{0,1:T(8,128)} %bitcast.2), kind=kLoop, calls=%fused_computation.46 | loop fusion | bytes 3407872 | tf_op jit(solution)/shard_map/slice | solution.py:235
  12.5 44.4 %transposed_product.1 = f32[13312,128]{1,0:T(8,128)} custom-call(s32[1]{0:T(128)} %bitcast.1.me_ref, f32[128,1664]{1,0:T(8,128)S(1)} %get-tuple-element.11.probe_ref, f32[1664,13312]{1,0:T(8,128)} %bitcast.3.matrix_ref), custom_call_target="tpu_custom_call" | custom-call | flops 22682796032 | bytes 88604672 | tf_op jit(solution)/shard_map/transposed_product/pallas_call | solution.py:72
  57.0 0.7 copy-done.1
  58.0 2.1 scatter_custom_fusion.1
  60.0 39.7 %all_to_all.24 = f32[8,96,256]{2,1,0:T(8,128)S(1)} all-to-all(f32[8,96,256]{2,1,0:T(8,128)S(1)} %bitcast.39), channel_id=1, replica_groups=mesh['front'=4,'blk'=8] {'blk'}, dimensions={0} | all-to-all | bytes 1572864 | tf_op jit(solution)/shard_map/all_to_all | solution.py:255
  99.8 1.5 collective-permute-start.1
  101.3 2.9 %scatter_custom_fusion = f32[768]{0:T(1024)S(1)} fusion(s32[384]{0:T(512)S(1)} %fusion.11, f32[384]{0:T(512)S(1)} %get-tuple-element.12, f32[]{:T(128)} %constant.59.clone.1), kind=kCustom, calls=%fused_computation.33 | custom fusion | bytes 3076 | tf_op jit(solution)/shard_map/scatter | solution.py:253
  104.2 0.7 all_to_all.16
  104.9 3.3 %all-to-all-start = ((f32[8,96,1]{1,2,0:T(1,128)}), f32[8,96,1]{1,2,0:T(1,128)S(1)}, u32[]{:S(2)}, u32[]{:S(2)}) async-start(f32[8,96,1]{1,2,0:T(1,128)} %bitcast.7), calls=%async_computation.1 | async-start | bytes 8192 | tf_op jit(solution)/shard_map/all_to_all | solution.py:256
  108.2 0.7 fusion.16
  109.6 4.0 %all-to-all-done = f32[8,96,1]{1,2,0:T(1,128)S(1)} async-done(((f32[8,96,1]{1,2,0:T(1,128)}), f32[8,96,1]{1,2,0:T(1,128)S(1)}, u32[]{:S(2)}, u32[]{:S(2)}) %all-to-all-start) | async-done | bytes 3104 | tf_op jit(solution)/shard_map/all_to_all | solution.py:256
  114.1 0.7 reduce.12
  114.9 1.7 collective-permute-start
  116.5 11.1 %gather_fusion.1 = f32[128,13312]{1,0:T(8,128)} fusion(f32[1664,13312]{1,0:T(8,128)} %bitcast.3.matrix_ref, s32[1024]{0:T(1024)S(1)} %pad_clamp_fusion.1), kind=kCustom, calls=%fused_computation.1 | custom fusion | bytes 13632000 | tf_op jit(solution)/shard_map/gather | solution.py:267
  127.6 7.6 %scatter_custom_fusion.2 = f32[1665,256]{1,0:T(8,128)} fusion(s32[768]{0:T(1024)S(1)} %convert_element_type.11, f32[768,256]{1,0:T(8,128)S(1)} %collective-permute-done.1, f32[]{:T(128)} %constant.58.clone.1), kind=kCustom, calls=%fused_computation.9 | custom fusion | flops 196608 | bytes 1704964 | tf_op jit(solution)/shard_map/scatter-add | solution.py:259
  135.2 8.4 %copy.17.probe_ref = f32[13312,128]{1,0:T(8,128)} copy(f32[13312,128]{0,1:T(8,128)} %all-gather.2.cloned.1.call-done) | data formatting | bytes 13631488 | tf_op jit(solution)/shard_map/all_gather | solution.py:235
  143.6 41.3 %forward_product.1 = f32[1664,128]{1,0:T(8,128)S(1)} custom-call(s32[1]{0:T(128)} %bitcast.1.me_ref, f32[13312,128]{1,0:T(8,128)} %copy.17.probe_ref, f32[1664,13312]{1,0:T(8,128)} %bitcast.3.matrix_ref), custom_call_target="tpu_custom_call" | custom-call | flops 22682796032 | bytes 88604672 | tf_op jit(solution)/shard_map/forward_product/pallas_call | solution.py:128
  184.9 1.8 slice_add_fusion.off_ref
  186.8 0.8 gather_fusion
  187.5 3.4 %fusion.upward_ref = f32[128,256]{1,0:T(8,128)S(1)} fusion(f32[128,256]{1,0:T(8,128)S(1)} %gather_fusion, f32[1664,256]{0,1:T(8,128)} %collective-permute-done.2, f32[128,13312]{1,0:T(8,128)} %gather_fusion.1, s32[]{:T(128)S(6)} %select_n.98, pred[128]{0:T(512)(128)(4,1)S(1)} %iota_compare_fusion.1), kind=kOutput, calls=%fused_computation.8 | convolution fusion | flops 654376960 | bytes 2818180 | tf_op jit(solution)/shard_map/dot_general | solution.py:27
  191.1 1.2 collective-permute-done.3
  192.4 0.8 gather_fusion.2
  193.1 20.0 %interpolate_both.1 = (f32[1664,128]{1,0:T(8,128)}, f32[128,128]{1,0:T(8,128)}) custom-call(s32[1]{0:T(128)} %bitcast.37.rank_ref, f32[1664,256]{1,0:T(8,128)S(1)} %slice_add_fusion.off_ref, f32[128,256]{1,0:T(8,128)S(1)} %broadcast_select_fusion.basis_ref, f32[128,256]{1,0:T(8,128)S(1)} %fusion.upward_ref, f32[128,256]{1,0:T(8,128)S(1)} %gather_fusion.2), custom_call_target="tpu_custom_call" | custom-call | tf_op jit(solution)/shard_map/interpolate_both/pallas_call | solution.py:209
  (30 shorter events, 1.3 us)
Async XLA Ops:
  7.2 50.8 %copy-start = (f32[1,384,256]{2,1,0:T(8,128)S(1)}, f32[1,384,256]{2,1,0:T(8,128)}, u32[]{:S(2)}) copy-start(f32[1,384,256]{2,1,0:T(8,128)} %param.9) | copy-start | bytes 1179652
  7.2 128.0 %all-gather.2.cloned.1.call-start = ((), (), s32[]{:S(2)}) async-start(), calls=%async_computation.3 | async-start | bytes 7667712 | tf_op jit(solution)/shard_map/all_gather | solution.py:235
  12.5 172.5 %reduce-scatter.2.cloned.1.call-start = ((), (), s32[]{:S(2)}) async-start(), calls=%async_computation.4 | async-start | bytes 7667712 | tf_op jit(solution)/shard_map/reduce_scatter | solution.py:237
  56.9 0.7 copy-start.1
  57.6 51.3 %copy-start.2 = (s32[1,1,128]{2,1,0:T(1,128)S(1)}, s32[1,1,128]{2,1,0:T(1,128)}, u32[]{:S(2)}) copy-start(s32[1,1,128]{2,1,0:T(1,128)} %param.11) | copy-start | bytes 1540
  99.8 27.8 %collective-permute-start.1 = (f32[768,256]{1,0:T(8,128)S(1)}, f32[768,256]{1,0:T(8,128)S(1)}, u32[]{:S(2)}, u32[]{:S(2)}) collective-permute-start(f32[768,256]{1,0:T(8,128)S(1)} %bitcast.40), channel_id=1, source_target_pairs={{0,8},{8,16},{16,24},{24,0},{1,9},{9,17},{17,25},{25,1},{2,10},{10... | collective-permute-start | bytes 2359304 | tf_op jit(solution)/shard_map/ppermute | solution.py:17
  101.3 86.3 %collective-permute-start.2 = (f32[1664,256]{0,1:T(8,128)}, f32[1664,256]{0,1:T(8,128)}, u32[]{:S(2)}, u32[]{:S(2)}) collective-permute-start(f32[1664,256]{0,1:T(8,128)} %bitcast.2), channel_id=1, source_target_pairs={{0,1},{1,0},{2,3},{3,2},{4,5},{5,4},{6,7},{7,6},{8,9},{9,8},{10,11... | collective-permute-start | bytes 5111816 | tf_op jit(solution)/shard_map/ppermute | solution.py:23
  104.9 8.8 %all-to-all-start = ((f32[8,96,1]{1,2,0:T(1,128)}), f32[8,96,1]{1,2,0:T(1,128)S(1)}, u32[]{:S(2)}, u32[]{:S(2)}) async-start(f32[8,96,1]{1,2,0:T(1,128)} %bitcast.7), calls=%async_computation.1 | async-start | bytes 8192 | tf_op jit(solution)/shard_map/all_to_all | solution.py:256
  114.9 12.7 %collective-permute-start = (f32[768]{0:T(1024)S(1)}, f32[768]{0:T(1024)S(1)}, u32[]{:S(2)}, u32[]{:S(2)}) collective-permute-start(f32[768]{0:T(1024)S(1)} %all_to_all.18), channel_id=1, source_target_pairs={{0,8},{8,16},{16,24},{24,0},{1,9},{9,17},{17,25},{25,1},{2,10},{10... | collective-permute-start | bytes 9224 | tf_op jit(solution)/shard_map/ppermute | solution.py:17
  190.9 1.4 collective-permute-start.3
Sparse Core Ops, SparseCore 0:
  12.6 86.7 all-gather.1
  101.6 73.6 reduce-scatter.1

commit v2 on v1

--- a/solution.py
+++ b/solution.py
@@ -234,7 +234,6 @@
 
     gathered = lax.all_gather(own_probe[:, :half], "blk", axis=0, tiled=True)
     partial = transposed_product(matrix, own_probe[:, half:].T, me)
-    upper_columns = lax.psum_scatter(partial, "blk", scatter_dimension=0, tiled=True)
     sibling_probe = from_partner(own_probe, "blk", 0)
 
     blocks = lax.axis_size("blk")
@@ -251,15 +250,6 @@
     slots_total = blocks * capacity
     sending = jnp.zeros((slots_total, samples), jnp.float32).at[places].set(incoming)
     labels = jnp.full((slots_total,), float(height), jnp.float32).at[places].set(within)
-    spread_rows, spread_labels = (
-        lax.all_to_all(sending, "blk", split_axis=0, concat_axis=0, tiled=True),
-        lax.all_to_all(labels, "blk", split_axis=0, concat_axis=0, tiled=True),
-    )
-    arrived, arrived_labels = from_behind((spread_rows, spread_labels), "front", 1)
-    child_part = jax.ops.segment_sum(
-        arrived, arrived_labels.astype(jnp.int32), num_segments=height + 1
-    )[:height]
-
     chosen = skeleton[0, 0]
     leaf_rank = leaf_ranks[0, 0]
     live_mask = (jnp.arange(chosen.shape[0]) < leaf_rank)[:, None]
@@ -267,7 +257,21 @@
     sibling_columns = lax.dynamic_slice_in_dim(matrix[chosen], sibling_start, height, 1)
     sibling_term = exact_dot(sibling_columns, sibling_probe)
 
+    sending, sibling_term, partial = lax.optimization_barrier((sending, sibling_term, partial))
+    upper_columns = lax.psum_scatter(partial, "blk", scatter_dimension=0, tiled=True)
+    spread_rows, spread_labels = (
+        lax.all_to_all(sending, "blk", split_axis=0, concat_axis=0, tiled=True),
+        lax.all_to_all(labels, "blk", split_axis=0, concat_axis=0, tiled=True),
+    )
+    arrived, arrived_labels = from_behind((spread_rows, spread_labels), "front", 1)
     lower_columns = forward_product(matrix, gathered, me)
+    arrived, arrived_labels, lower_columns = lax.optimization_barrier(
+        (arrived, arrived_labels, lower_columns)
+    )
+    child_part = jax.ops.segment_sum(
+        arrived, arrived_labels.astype(jnp.int32), num_segments=height + 1
+    )[:height]
+
     off_sample = jnp.concatenate([lower_columns, upper_columns], axis=1) + child_part
     picked = off_sample[chosen]
     leaf_basis = jnp.where(live_mask, picked, 0.0)

time: 221 us -> 207 us (0.937)
  blocking collectives: 39.7 us -> 11.4 us
  waiting for transfers between devices: 5.35 us -> 31.1 us
  local copies, waits for them, and re-layouts: 33 us -> 22 us
    all_to_all x1, blocking collectives: 39.7 us -> 11.4 us  [body(): lax.all_to_all(labels, 'blk', split_axis=0, concat_axis=0, tiled=True)]
    all_to_all x1, waiting for transfers between devices: 4.05 us -> 30.4 us  [body(): lax.all_to_all(sending, 'blk', split_axis=0, concat_axis=0, tiled=True)]
    all_gather x1 -> x0, local copies, waits for them, and re-layouts: 8.38 us -> none  [body(): gathered = lax.all_gather(own_probe[:, :half], 'blk', axis=0, tiled=True)]
    unnamed x7 -> x6, local copies, waits for them, and re-layouts: 3.45 us -> 0.02 us
  transfers between devices with their start and end apart: 7 -> 7, of which waited for: 2 -> 2; matrix products, arithmetic and copies ran while one was open for 17% -> 14% of each run, Pallas kernels for 39% -> 41%
where the time goes in v2:
time: 207 us; the launch traced here: 206 us
  Pallas kernels  105 us (51%)
  waiting for transfers between devices  31.1 us (15%)
  local copies, waits for them, and re-layouts  22 us (11%)
  between operations  14.9 us (7%)
  blocking collectives  11.4 us (6%)
  other arithmetic  11.2 us (5%)
  starting transfers between devices  7.1 us (3%)
  matrix products  2.69 us (1%)
    pallas_call x1, Pallas kernels, transposed_product(): pl.pallas_call(functools.partial(transposed_kernel, height, sub), grid=(w...  44 us
    pallas_call x1, Pallas kernels, forward_product(): pl.pallas_call(functools.partial(forward_kernel, height, chunk), grid=(wi...  41.4 us
    all_to_all x1, waiting for transfers between devices, body(): lax.all_to_all(sending, 'blk', split_axis=0, concat_axis=0, tiled=True)  30.4 us
    pallas_call x1, Pallas kernels, interpolate_both(): pl.pallas_call(interpolate_kernel, in_specs=[pl.BlockSpec(memory_space=pl...  20 us
    all_to_all x1, blocking collectives, body(): lax.all_to_all(labels, 'blk', split_axis=0, concat_axis=0, tiled=True)  11.4 us
    gather x1, local copies, waits for them, and re-layouts, body(): matrix[chosen]  11.3 us
    scatter-add x1, other arithmetic, body(): jax.ops.segment_sum(arrived, arrived_labels.astype(jnp.int32), num_segmen...  7.56 us
  transfers between devices with their start and end apart: 7, of which 2 were waited for; matrix products, arithmetic and copies ran while one was open for 14% of the time, Pallas kernels for 41%

profile of v2, /device:TPU:0, one launch (start us, length us, event | category | flops | bytes accessed | tf_op | source)
XLA Modules:
  0.0 205.7 jit_solution(12743718845408267401)
XLA Ops:
  7.2 2.5 %fusion.18 = (f32[1664,128]{1,0:T(8,128)}, f32[128,1664]{0,1:T(8,128)S(1)}) fusion(f32[1664,256]{1,0:T(8,128)} %bitcast.7), kind=kLoop, calls=%fused_computation.46 | loop fusion | bytes 3407872 | tf_op jit(solution)/shard_map/slice | solution.py:235
  9.8 0.5 collective-permute-start
  10.3 0.3 copy.13.probe_ref
  10.6 11.3 %gather_fusion = f32[128,13312]{1,0:T(8,128)} fusion(f32[1664,13312]{1,0:T(8,128)} %bitcast.4.matrix_ref, s32[1024]{0:T(1024)S(1)} %pad_clamp_fusion.1), kind=kCustom, calls=%fused_computation | custom fusion | bytes 13632000 | tf_op jit(solution)/shard_map/gather | solution.py:257
  22.0 0.2 convert_reduce_fusion
  22.3 2.8 %scatter_custom_fusion = f32[768,256]{1,0:T(8,128)} fusion(s32[384]{0:T(512)S(1)} %fusion.11, f32[1,384,256]{2,1,0:T(8,128)S(1)} %copy-done, f32[]{:T(128)} %constant.57.clone.1), kind=kCustom, calls=%fused_computation.15 | custom fusion | bytes 1179652 | tf_op jit(solution)/shard_map/scatter | solution.py:251
  25.1 44.0 %transposed_product.1 = f32[13312,128]{1,0:T(8,128)} custom-call(s32[1]{0:T(128)} %bitcast.8.me_ref, f32[128,1664]{1,0:T(8,128)S(1)} %copy.13.probe_ref, f32[1664,13312]{1,0:T(8,128)} %bitcast.4.matrix_ref), custom_call_target="tpu_custom_call" | custom-call | flops 22682796032 | bytes 88604672 | tf_op jit(solution)/shard_map/transposed_product/pallas_call | solution.py:72
  69.0 2.7 %fusion.2 = f32[128,256]{1,0:T(8,128)S(1)} fusion(f32[1664,256]{1,0:T(8,128)} %collective-permute-done, f32[128,13312]{1,0:T(8,128)} %gather_fusion, s32[]{:T(128)S(6)} %select_n.96), kind=kOutput, calls=%fused_computation.10 | convolution fusion | flops 654311424 | bytes 2686980 | tf_op jit(solution)/shard_map/dot_general | solution.py:27
  71.7 2.9 %scatter_custom_fusion.1 = f32[768]{0:T(1024)S(1)} fusion(s32[384]{0:T(512)S(1)} %fusion.11, f32[384]{0:T(512)S(1)} %get-tuple-element.26, f32[]{:T(128)} %constant.66.clone.1), kind=kCustom, calls=%fused_computation.33 | custom fusion | bytes 3076 | tf_op jit(solution)/shard_map/scatter | solution.py:252
  74.7 11.4 %all_to_all.24 = f32[8,96,1]{1,2,0:T(1,128)S(1)} all-to-all(f32[8,96,1]{1,2,0:T(1,128)S(1)} %bitcast.40), channel_id=1, replica_groups=mesh['front'=4,'blk'=8] {'blk'}, dimensions={0} | all-to-all | bytes 6144 | tf_op jit(solution)/shard_map/all_to_all | solution.py:264
  86.2 3.6 %all-to-all-start = ((f32[8,96,256]{2,1,0:T(8,128)}), f32[8,96,256]{2,1,0:T(8,128)S(1)}, u32[]{:S(2)}, u32[]{:S(2)}) async-start(f32[8,96,256]{2,1,0:T(8,128)} %bitcast.10), calls=%async_computation | async-start | bytes 1572864 | tf_op jit(solution)/shard_map/all_to_all | solution.py:263
  90.4 0.5 broadcast.172
  91.0 0.7 reduce.12
  91.7 1.4 collective-permute-start.2
  93.1 30.4 %all-to-all-done = f32[8,96,256]{2,1,0:T(8,128)S(1)} async-done(((f32[8,96,256]{2,1,0:T(8,128)}), f32[8,96,256]{2,1,0:T(8,128)S(1)}, u32[]{:S(2)}, u32[]{:S(2)}) %all-to-all-start) | async-done | bytes 786464 | tf_op jit(solution)/shard_map/all_to_all | solution.py:263
  123.5 1.4 collective-permute-start.1
  124.9 41.4 %forward_product.1 = f32[1664,128]{1,0:T(8,128)S(1)} custom-call(s32[1]{0:T(128)} %bitcast.8.me_ref, f32[13312,128]{1,0:T(8,128)} %all-gather.2.cloned.1.call-done.probe_ref, f32[1664,13312]{1,0:T(8,128)} %bitcast.4.matrix_ref), custom_call_target="tpu_custom_call" | custom-call | flops 22682796032 | bytes 88604672 | tf_op jit(solution)/shard_map/forward_product/pallas_call | solution.py:128
  166.3 7.6 %scatter_custom_fusion.2 = f32[1665,256]{1,0:T(8,128)} fusion(s32[768]{0:T(1024)S(1)} %convert_element_type.11, f32[768,256]{1,0:T(8,128)S(1)} %collective-permute-done.1, f32[]{:T(128)} %constant.57.clone.1), kind=kCustom, calls=%fused_computation.7 | custom fusion | flops 196608 | bytes 1704964 | tf_op jit(solution)/shard_map/scatter-add | solution.py:271
  173.9 1.8 slice_add_fusion.off_ref
  175.7 0.8 gather_fusion.1
  176.6 0.7 fusion.16
  177.3 0.6 collective-permute-done.3
  178.0 0.8 gather_fusion.2
  178.8 20.0 %interpolate_both.1 = (f32[1664,128]{1,0:T(8,128)}, f32[128,128]{1,0:T(8,128)}) custom-call(s32[1]{0:T(128)} %bitcast.37.rank_ref, f32[1664,256]{1,0:T(8,128)S(1)} %slice_add_fusion.off_ref, f32[128,256]{1,0:T(8,128)S(1)} %get-tuple-element.25.basis_ref, f32[128,256]{1,0:T(8,128)S(1)} %get-tuple-element.24.upward_ref, f32[128,256]{1,0:T(8,128)S(1)} %gather_fusion.2), custom_call_target="tpu_custom_call" | custom-call | tf_op jit(solution)/shard_map/interpolate_both/pallas_call | solution.py:209
  (29 shorter events, 0.6 us)
Async XLA Ops:
  7.2 15.1 %copy-start = (f32[1,384,256]{2,1,0:T(8,128)S(1)}, f32[1,384,256]{2,1,0:T(8,128)}, u32[]{:S(2)}) copy-start(f32[1,384,256]{2,1,0:T(8,128)} %param.9) | copy-start | bytes 1179652
  7.2 117.7 %all-gather.2.cloned.1.call-start = ((), (), s32[]{:S(2)}) async-start(), calls=%async_computation.3 | async-start | bytes 7667712 | tf_op jit(solution)/shard_map/all_gather | solution.py:235
  9.7 0.9 copy-start.2
  9.7 164.2 %reduce-scatter.2.cloned.1.call-start = ((), (), s32[]{:S(2)}) async-start(), calls=%async_computation.4 | async-start | bytes 7667712 | tf_op jit(solution)/shard_map/reduce_scatter | solution.py:261
  9.8 59.3 %collective-permute-start = (f32[1664,256]{1,0:T(8,128)}, f32[1664,256]{1,0:T(8,128)}, u32[]{:S(2)}, u32[]{:S(2)}) collective-permute-start(f32[1664,256]{1,0:T(8,128)} %bitcast.7), channel_id=1, source_target_pairs={{0,1},{1,0},{2,3},{3,2},{4,5},{5,4},{6,7},{7,6},{8,9},{9,8},{10,11... | collective-permute-start | bytes 5111816 | tf_op jit(solution)/shard_map/ppermute | solution.py:23
  10.6 11.3 %copy-start.1 = (s32[1,384]{1,0:T(1,128)S(1)}, s32[1,384]{1,0:T(1,128)}, u32[]{:S(2)}) copy-start(s32[1,384]{1,0:T(1,128)} %param.10) | copy-start | bytes 4612
  86.2 37.3 %all-to-all-start = ((f32[8,96,256]{2,1,0:T(8,128)}), f32[8,96,256]{2,1,0:T(8,128)S(1)}, u32[]{:S(2)}, u32[]{:S(2)}) async-start(f32[8,96,256]{2,1,0:T(8,128)} %bitcast.10), calls=%async_computation | async-start | bytes 1572864 | tf_op jit(solution)/shard_map/all_to_all | solution.py:263
  91.7 74.6 %collective-permute-start.2 = (f32[768]{0:T(1024)S(1)}, f32[768]{0:T(1024)S(1)}, u32[]{:S(2)}, u32[]{:S(2)}) collective-permute-start(f32[768]{0:T(1024)S(1)} %all_to_all.21), channel_id=1, source_target_pairs={{0,8},{8,16},{16,24},{24,0},{1,9},{9,17},{17,25},{25,1},{2,10},{10... | collective-permute-start | bytes 9224 | tf_op jit(solution)/shard_map/ppermute | solution.py:17
  123.5 42.8 %collective-permute-start.1 = (f32[768,256]{1,0:T(8,128)S(1)}, f32[768,256]{1,0:T(8,128)S(1)}, u32[]{:S(2)}, u32[]{:S(2)}) collective-permute-start(f32[768,256]{1,0:T(8,128)S(1)} %bitcast.39), channel_id=1, source_target_pairs={{0,8},{8,16},{16,24},{24,0},{1,9},{9,17},{17,25},{25,1},{2,10},{10... | collective-permute-start | bytes 2359304 | tf_op jit(solution)/shard_map/ppermute | solution.py:17
  176.6 1.4 collective-permute-start.3
Sparse Core Ops, SparseCore 0:
  10.2 71.7 all-gather.1
  84.4 85.9 reduce-scatter.1
